TPU v7x, 32 devices: a whole 2x2x4 slice. The times are simulated.
32 devices in a mesh: blk: 16 (over z, y, x), head: 2 (over core).
Axes of the slice: x: 2, y: 2, z: 4, core: 2. Of those that a mesh axis runs over, the one named last changes fastest.
Arguments:
- vision: bfloat16 [16, 1601, 8192], P('blk', None, 'head'), may hold values from -6 to 6
- kept_index: int32 [16, 128], P('blk'), may hold values from 0 to 1600, as said below
- w_key: bfloat16 [8192, 1024], P('head', 'blk'), may hold values from -0.0625 to 0.0625
- w_value: bfloat16 [8192, 1024], P('head', 'blk'), may hold values from -0.0625 to 0.0625
- queries: bfloat16 [2048, 8192], P('blk', 'head'), may hold values from -140 to 140
- last_frame: int32 [2048], P('blk'), may hold values from 0 to 15, as said below
- attn_gate: float32 [1], replicated, may hold values from 0.3 to 1.5
Outputs:
- gated: bfloat16 [2048, 8192], P('blk', 'head')
Inputs may be any that keep to these rules, and one draw needn't show every extreme that they name: `kept_index`: each frame's indices are distinct; index 0 (the class token) and index 1600 are kept in every frame. `last_frame`: never falls from one row to the next; row 0 sees only frame 0, the last row sees all frames, and every frame is the last frame of at least one row.
All inputs are finite; a program needn't handle non-finite values.
Results may differ from a plain program's by a relative error of at most 0.012.
The roundings to bfloat16 on the way count: a program that leaves them out, or rounds other values in their place, can miss the bound.
Values may be sent and summed in bfloat16 or wider, within the bound.
A program may use at most 128 MiB of HBM per device.

v0:
```python
import jax
import jax.numpy as jnp
from jax import lax
from jax.sharding import PartitionSpec as P

HD = 128


def fold_frames(running, query_heads, last_rows, key_piece, value_piece):
    row_max, denominator, numerator = running
    frames_here = key_piece.shape[0]
    scores = jnp.einsum(
        "rkgd,fjkd->rkgfj", query_heads, key_piece, preferred_element_type=jnp.float32
    ) * HD ** (-0.5)
    frame_ids = jnp.arange(frames_here, dtype=jnp.int32)
    visible = frame_ids[None, :] <= last_rows[:, None]
    scores = jnp.where(visible[:, None, None, :, None], scores, jnp.float32(-1e30))
    new_max = jnp.maximum(row_max, jnp.max(scores, axis=(3, 4)))
    exps = jnp.exp(scores - new_max[..., None, None])
    new_denominator = jnp.sum(exps, axis=(3, 4))
    weights = exps.astype(jnp.bfloat16)
    added = jnp.einsum("rkgfj,fjkd->rkgd", weights, value_piece, preferred_element_type=jnp.float32)
    return (new_max, new_denominator, added)


def attend(rows_q, rows_last, groups, key_rows, value_rows, attn_gate):
    total_rows, row_width = rows_q.shape
    local_kv = key_rows.shape[2] // HD
    group_size = row_width // HD // local_kv
    group_rows = total_rows // groups
    query_groups = [rows_q.reshape(group_rows, local_kv, group_size, HD)]
    last_groups = [rows_last]
    initial = tuple(
        (
            (
                jnp.full((group_rows, local_kv, group_size), -1e30, jnp.float32),
                jnp.zeros((group_rows, local_kv, group_size), jnp.float32),
                jnp.zeros((group_rows, local_kv, group_size, HD), jnp.float32),
            )
            for member in range(groups)
        )
    )
    key_piece = lax.all_gather(key_rows, "blk", axis=0, tiled=True)
    value_piece = lax.all_gather(value_rows, "blk", axis=0, tiled=True)
    frames_here = key_piece.shape[0]
    key_piece = key_piece.reshape(frames_here, key_piece.shape[1], local_kv, HD)
    value_piece = value_piece.reshape(frames_here, value_piece.shape[1], local_kv, HD)
    member = 0
    query_heads = query_groups[member]
    last_rows = last_groups[member]
    state_new = fold_frames(initial[member], query_heads, last_rows, key_piece, value_piece)
    updated = [state_new]
    results = tuple(updated)
    gate_factor = jnp.tanh(attn_gate[0])
    pieces_out = [
        (gate_factor * (numerator / denominator[..., None])).reshape(group_rows, row_width)
        for row_max, denominator, numerator in results
    ]
    return pieces_out[0].astype(jnp.bfloat16)


def local(vision, kept_index, w_key, w_value, queries, last_frame, attn_gate):
    chosen = vision[0][kept_index[0]]
    stacked = jnp.stack([w_key, w_value])
    partial_value = jnp.einsum(
        "td,sdc->stc",
        chosen,
        lax.all_gather(stacked, "blk", axis=2, tiled=True),
        preferred_element_type=jnp.float32,
    )
    summed = lax.psum_scatter(partial_value, "head", scatter_dimension=2, tiled=True).astype(
        jnp.bfloat16
    )
    key_rows = summed[0][None]
    value_rows = summed[1][None]
    return attend(queries, last_frame, 1, key_rows, value_rows, attn_gate)


def solution(mesh):
    in_specs = (
        P("blk", None, "head"),
        P("blk", None),
        P("head", "blk"),
        P("head", "blk"),
        P("blk", "head"),
        P("blk"),
        P(),
    )
    out_specs = P("blk", "head")
    return jax.shard_map(local, mesh=mesh, in_specs=in_specs, out_specs=out_specs, check_vma=False)
```

profile of v0, /device:TPU:0, one launch (start us, length us, event | category | flops | bytes accessed | tf_op | source)
XLA Modules:
  0.0 367.1 jit_solution(5283368969549839552)
XLA Ops:
  6.5 2.3 pad_maximum_fusion
  8.8 0.0 all-gather.4.cloned.1.call-update
  8.8 0.0 reduce-scatter.2.cloned.1.call-start
  8.9 0.7 fusion.16
  9.6 8.7 %gather_fusion = bf16[128,4096]{1,0:T(8,128)(2,1)S(1)} fusion(bf16[1601,4096]{1,0:T(8,128)(2,1)} %bitcast.44, s32[1024]{0:T(1024)S(1)} %pad_clamp_fusion), kind=kCustom, calls=%fused_computation | custom fusion | bytes 2097664 | tf_op jit(solution)/shard_map/gather | solution.py:63
  18.3 186.2 %all-gather.4.cloned.1.call-done = bf16[2,4096,1024]{1,2,0:T(8,128)(2,1)} async-done(((bf16[2,4096,64]{1,2,0:T(8,128)(2,1)}), bf16[2,4096,1024]{1,2,0:T(8,128)(2,1)}) %all-gather.4.cloned.1.call-update) | async-done | bytes 16777232 | tf_op jit(solution)/shard_map/all_gather | solution.py:68
  204.5 9.1 %convolution_bitcast_fusion = f32[2,128,1024]{1,2,0:T(8,128)} fusion(bf16[2,4096,1024]{1,2,0:T(8,128)(2,1)} %all-gather.4.cloned.1.call-done, bf16[128,4096]{1,0:T(8,128)(2,1)S(1)} %gather_fusion), kind=kOutput, calls=%fused_computation.14 | convolution fusion | flops 2147483648 | bytes 18874368 | tf_op jit(solution)/shard_map/td,sdc->stc/dot_general | solution.py:65
  213.6 0.0 reduce-scatter.2.cloned.1.call-update
  213.7 0.0 all-gather.8.cloned.1.call-start
  213.7 6.8 %reduce-scatter.2.cloned.1.call-done = f32[2,128,512]{1,2,0:T(8,128)} async-done(((f32[2,128,1024]{1,2,0:T(8,128)}), f32[2,128,512]{1,2,0:T(8,128)}) %reduce-scatter.2.cloned.1.call-update) | async-done | bytes 524304 | tf_op jit(solution)/shard_map/reduce_scatter | solution.py:71
  220.6 1.1 convert_element_type.12
  221.7 0.8 copy.20
  222.4 0.0 all-gather.8.cloned.1.call-update
  222.5 0.2 all-gather.6.cloned.1.call-start
  222.7 0.2 copy.39
  223.7 0.8 copy.18
  224.5 61.1 %all-gather.8.cloned.1.call-done = bf16[16,128,512]{2,1,0:T(8,128)(2,1)} async-done(((bf16[1,128,512]{2,1,0:T(8,128)(2,1)}), bf16[16,128,512]{2,1,0:T(8,128)(2,1)}) %all-gather.8.cloned.1.call-update) | async-done | bytes 2097168 | tf_op jit(solution)/shard_map/all_gather | solution.py:43
  285.6 3.0 copy.21
  288.6 13.5 %fusion.2 = (f32[128,4,8]{0,2,1:T(8,128)S(1)}, f32[4,16,128,128,8]{3,2,4,1,0:T(8,128)}) fusion(pred[128,16]{0,1:T(8,128)(4,1)S(1)} %iota_compare_fusion, bf16[128,4,8,128,1]{3,2,1,0,4:T(8,128)(2,1)S(1)} %bitcast.45, bf16[16,128,4,128,1]{1,3,2,0,4:T(8,128)(2,1)S(1)} %bitcast.43), kind=kOutput, calls=%fused_computation.5 | convolution fusion | flops 2172645376 | bytes 36718592 | tf_op jit(solution)/shard_map/rkgd,fjkd->rkgfj/dot_general | solution.py:12
  302.2 20.0 %fusion.1 = (bf16[128,4,8,16,128]{0,4,2,3,1:T(8,128)(2,1)}, f32[128,4,8]{0,2,1:T(8,128)S(1)}) fusion(f32[4,16,128,128,8]{3,2,4,1,0:T(8,128)} %get-tuple-element.10, f32[128,4,8]{0,2,1:T(8,128)S(1)} %broadcast_maximum_fusion, pred[128,16]{0,1:T(8,128)(4,1)S(1)} %iota_compare_fusion), kind=kLoop, calls=%fused_computation.4 | loop fusion | flops 41938944 | bytes 50366464 | tf_op jit(solution)/shard_map/convert_element_type | solution.py:21
  322.2 25.8 %all-gather.6.cloned.1.call-done = bf16[16,128,512]{2,1,0:T(8,128)(2,1)} async-done(((bf16[1,128,512]{2,1,0:T(8,128)(2,1)}), bf16[16,128,512]{2,1,0:T(8,128)(2,1)}) %all-gather.6.cloned.1.call-update) | async-done | bytes 2097168 | tf_op jit(solution)/shard_map/all_gather | solution.py:44
  348.0 3.0 copy.19
  351.0 8.2 %fusion.6 = bf16[128,4,8,128]{0,3,2,1:T(8,128)(2,1)S(1)} fusion(f32[128,4,8]{0,2,1:T(8,128)S(1)} %get-tuple-element.6, f32[]{:T(128)} %bitcast, bf16[128,4,8,16,128]{0,4,2,3,1:T(8,128)(2,1)} %get-tuple-element.5, bf16[16,128,4,128,1]{1,3,2,0,4:T(8,128)(2,1)S(1)} %bitcast.46), kind=kOutput, calls=%fused_computation.10 | convolution fusion | flops 2149056512 | bytes 19939332 | tf_op jit(solution)/shard_map/rkgfj,fjkd->rkgd/dot_general | solution.py:22
  359.2 1.3 copy.26
  (10 shorter events, 0.1 us)
Async XLA Ops:
  6.5 198.0 %all-gather.4.cloned.1.call-start = ((), (), s32[]{:S(2)}) async-start(), calls=%async_computation.1 | async-start | bytes 17825792 | tf_op jit(solution)/shard_map/all_gather | solution.py:68
  8.8 211.7 %reduce-scatter.2.cloned.1.call-start = ((), (), s32[]{:S(2)}) async-start(), calls=%async_computation.2 | async-start | bytes 1572864 | tf_op jit(solution)/shard_map/reduce_scatter | solution.py:71
  9.5 213.1 %copy-start = (bf16[128,4096]{1,0:T(8,128)(2,1)S(1)}, bf16[128,4096]{1,0:T(8,128)(2,1)}, u32[]{:S(2)}) copy-start(bf16[128,4096]{1,0:T(8,128)(2,1)} %param.11) | copy-start | bytes 3145732
  18.3 205.4 %copy-start.1 = (s32[128]{0:T(128)S(1)}, s32[128]{0:T(128)}, u32[]{:S(2)}) copy-start(s32[128]{0:T(128)} %param.12) | copy-start | bytes 1540
  213.7 71.9 %all-gather.8.cloned.1.call-start = ((), (), s32[]{:S(2)}) async-start(), calls=%async_computation.4 | async-start | bytes 2228224 | tf_op jit(solution)/shard_map/all_gather | solution.py:43
  222.5 125.5 %all-gather.6.cloned.1.call-start = ((), (), s32[]{:S(2)}) async-start(), calls=%async_computation.3 | async-start | bytes 2228224 | tf_op jit(solution)/shard_map/all_gather | solution.py:44
Sparse Core Ops, SparseCore 0:
  10.1 194.3 all-gather.3
  213.8 6.7 reduce-scatter.1
  223.7 61.8 all-gather.7
  288.6 59.3 all-gather.5
where the time goes:
time: 368 us; the launch traced here: 367 us
  waiting for transfers between devices  280 us (76%)
  matrix products  30.8 us (8%)
  other arithmetic  24 us (7%)
  local copies, waits for them, and re-layouts  17.9 us (5%)
  between operations  13.9 us (4%)
    all_gather x1, waiting for transfers between devices, local(): lax.all_gather(stacked, 'blk', axis=2, tiled=True)  186 us
    all_gather x1, waiting for transfers between devices, attend(): key_piece = lax.all_gather(key_rows, 'blk', axis=0, tiled=True)  61.1 us
    all_gather x1, waiting for transfers between devices, attend(): value_piece = lax.all_gather(value_rows, 'blk', axis=0, tiled=True)  25.8 us
    convert_element_type x1, other arithmetic, fold_frames(): weights = exps.astype(jnp.bfloat16)  20 us
    dot_general x1, matrix products, fold_frames(): jnp.einsum('rkgd,fjkd->rkgfj', query_heads, key_piece, preferred_element_...  13.5 us
    dot_general x1, matrix products, local(): jnp.einsum('td,sdc->stc', chosen, lax.all_gather(stacked, 'blk', axis=2,...  9.09 us
    gather x1, local copies, waits for them, and re-layouts, local(): chosen = vision[0][kept_index[0]]  8.73 us
    dot_general x1, matrix products, fold_frames(): jnp.einsum('rkgfj,fjkd->rkgd', weights, value_piece, preferred_element_ty...  8.21 us
  transfers between devices with their start and end apart: 4, of which 4 were waited for; matrix products, arithmetic and copies ran while one was open for 13% of the time, Pallas kernels for 0%

commit v1 on v0

--- a/solution.py
+++ b/solution.py
@@ -1,9 +1,311 @@
 import jax
 import jax.numpy as jnp
 from jax import lax
+from jax.experimental import pallas as pl
+from jax.experimental.pallas import tpu as pltpu
 from jax.sharding import PartitionSpec as P
 
 HD = 128
+MESH = pl.DeviceIdType.MESH
+PIECES = 8
+STACK = 2
+
+
+def fused_kernel(
+    vision_ref, tail_ref, index_ref, w_key_ref, w_value_ref, q_ref, last_ref, gate_ref, out_ref,
+    vision_buf, onehot, chosen, weights, sums, partner_sums, kv, q_all, last_all, bias, out_parts,
+    vision_sem, w_send, w_recv, c_send, c_recv, q_send, q_recv, l_send, l_recv,
+    s_send, s_recv, kv_send, kv_recv, o_send, o_recv,
+):
+    blk = lax.axis_index("blk")
+    side = lax.axis_index("head")
+    z1, member, x = blk // 8, (blk % 8) // 2, blk % 2
+    z0, y = member // 2, member % 2
+    frame_at = lambda zz, mm, xx: zz * 8 + mm * 2 + xx
+    to_x = (frame_at(z1, member, 1 - x), side)
+    to_z1 = (frame_at(1 - z1, member, x), side)
+    to_y = (frame_at(z1, z0 * 2 + 1 - y, x), side)
+    to_z0 = (frame_at(z1, (1 - z0) * 2 + y, x), side)
+    to_diagonal = (frame_at(z1, (1 - z0) * 2 + 1 - y, x), side)
+    to_core = (blk, 1 - side)
+    partners = (to_x, to_z1, to_y, to_z0, to_diagonal, to_core)
+
+    def send(src, dst, send_sem, recv_sem, device):
+        return pltpu.make_async_remote_copy(
+            src_ref=src, dst_ref=dst, send_sem=send_sem, recv_sem=recv_sem,
+            device_id=device, device_id_type=MESH,
+        )
+
+    depth = chosen.shape[3]
+    main_rows = vision_buf.shape[1]
+
+    def vision_copy(k):
+        columns = pl.ds(pl.multiple_of(k * depth, depth), depth)
+        slot = lax.rem(k, 2)
+        return pltpu.make_async_copy(
+            vision_ref.at[0, pl.ds(0, main_rows), columns], vision_buf.at[slot], vision_sem.at[slot]
+        )
+
+    def w_copy(kind, k):
+        slot = weights.at[k, z1 if kind < 2 else 1 - z1, x]
+        return send(slot, slot, w_send.at[kind, k], w_recv.at[kind, k], to_z1 if kind == 1 else to_x)
+
+    def w_arrival(kind, k):
+        slot = weights.at[k, z1 if kind == 0 else 1 - z1, x if kind == 1 else 1 - x]
+        return send(slot, slot, w_send.at[kind, k], w_recv.at[kind, k], to_x)
+
+    def c_copy(kind, k):
+        slot = chosen.at[k, member if kind < 2 else (1 - z0) * 2 + y]
+        return send(slot, slot, c_send.at[kind, k], c_recv.at[kind, k], to_z0 if kind == 1 else to_y)
+
+    def c_arrival(kind, k):
+        from_z0 = z0 if kind == 0 else 1 - z0
+        from_y = y if kind == 1 else 1 - y
+        slot = chosen.at[k, from_z0 * 2 + from_y]
+        return send(slot, slot, c_send.at[kind, k], c_recv.at[kind, k], to_y)
+
+    def kv_copy(kind, j):
+        slot = kv.at[frame_at(z1 if kind < 2 else 1 - z1, j, x)]
+        return send(slot, slot, kv_send.at[kind, j], kv_recv.at[kind, j], to_z1 if kind == 1 else to_x)
+
+    def kv_arrival(kind, j):
+        slot = kv.at[frame_at(z1 if kind == 0 else 1 - z1, j, x if kind == 1 else 1 - x)]
+        return send(slot, slot, kv_send.at[kind, j], kv_recv.at[kind, j], to_x)
+
+    width = q_all.shape[2]
+
+    def peer(t):
+        return lax.rem(member + t, 4)
+
+    def columns_of(m):
+        return pl.ds(pl.multiple_of(m * width, width), width)
+
+    def q_copy(t):
+        target = (frame_at(z1, peer(t), x), side)
+        return send(q_ref.at[:, columns_of(peer(t))], q_all.at[member], q_send.at[t], q_recv.at[t], target)
+
+    def q_arrival(t):
+        slot = q_all.at[peer(4 - t)]
+        return send(slot, slot, q_send.at[t], q_recv.at[t], to_y)
+
+    def l_copy(t):
+        target = (frame_at(z1, peer(t), x), side)
+        return send(last_all.at[member], last_all.at[member], l_send.at[t], l_recv.at[t], target)
+
+    def l_arrival(t):
+        slot = last_all.at[peer(4 - t)]
+        return send(slot, slot, l_send.at[t], l_recv.at[t], to_y)
+
+    def o_copy(t):
+        target = (frame_at(z1, peer(t), x), side)
+        return send(out_parts.at[t], out_ref.at[:, columns_of(member)], o_send.at[t], o_recv.at[t], target)
+
+    def o_arrival(t):
+        slot = out_ref.at[:, columns_of(peer(4 - t))]
+        return send(slot, slot, o_send.at[t], o_recv.at[t], to_y)
+
+    def s_copy(j):
+        return send(sums.at[1 - side, j], partner_sums.at[j], s_send.at[j], s_recv.at[j], to_core)
+
+    vision_copy(0).start()
+    vision_copy(1).start()
+
+    def join_weights(k, carry):
+        rows = pl.ds(pl.multiple_of(k * depth, depth), depth)
+        weights[k, z1, x] = jnp.concatenate([w_key_ref[rows, :], w_value_ref[rows, :]], axis=1)
+        return carry
+
+    lax.fori_loop(0, PIECES, join_weights, 0)
+
+    barrier = pltpu.get_barrier_semaphore()
+    for device in partners:
+        pl.semaphore_signal(barrier, inc=1, device_id=device, device_id_type=MESH)
+    pl.semaphore_wait(barrier, len(partners))
+
+    def send_weights(k, carry):
+        w_copy(1, k).start()
+        w_copy(0, k).start()
+        return carry
+
+    lax.fori_loop(0, PIECES, send_weights, 0)
+
+    index_rows = jnp.broadcast_to(index_ref[...], (HD, HD)).T
+    lanes = lax.broadcasted_iota(jnp.int32, (HD, HD), 1)
+    for block in range(main_rows // HD):
+        onehot[:, block * HD:(block + 1) * HD] = jnp.where(
+            index_rows == lanes + block * HD, 1.0, 0.0
+        ).astype(jnp.bfloat16)
+    tail_start = vision_ref.shape[1] - HD
+    tail_rows = lanes + tail_start
+    onehot[:, main_rows:] = jnp.where(
+        (index_rows == tail_rows) & (tail_rows >= main_rows), 1.0, 0.0
+    ).astype(jnp.bfloat16)
+
+    def choose(k, carry):
+        vision_copy(k).wait()
+        columns = pl.ds(pl.multiple_of(k * depth, depth), depth)
+        picked = jnp.dot(
+            onehot[:, :main_rows], vision_buf[lax.rem(k, 2)], preferred_element_type=jnp.float32
+        ) + jnp.dot(
+            onehot[:, main_rows:], tail_ref[:, columns], preferred_element_type=jnp.float32
+        )
+        chosen[k, member] = picked.astype(jnp.bfloat16)
+        c_copy(1, k).start()
+        c_copy(0, k).start()
+
+        @pl.when(k + 2 < PIECES)
+        def _():
+            vision_copy(k + 2).start()
+
+        return carry
+
+    lax.fori_loop(0, PIECES, choose, 0)
+
+    last_all[member] = jnp.broadcast_to(last_ref[...], (8, HD))
+    q_all[member] = q_ref[:, columns_of(member)]
+    for t in (1, 2, 3):
+        l_copy(t).start()
+        q_copy(t).start()
+
+    def relay(k, carry):
+        w_arrival(1, k).wait_recv()
+        w_copy(2, k).start()
+        c_arrival(1, k).wait_recv()
+        c_copy(2, k).start()
+        return carry
+
+    lax.fori_loop(0, PIECES, relay, 0)
+
+    sums[...] = jnp.zeros_like(sums)
+
+    def project(k, carry):
+        for kind in (0, 2):
+            w_arrival(kind, k).wait_recv()
+            c_arrival(kind, k).wait_recv()
+        rows = chosen[k].reshape(4 * HD, depth)
+        for group in range(2):
+            columns = jnp.concatenate([weights[k, group, 0], weights[k, group, 1]], axis=1)
+            added = jnp.dot(rows, columns, preferred_element_type=jnp.float32)
+            sums[group] += added.reshape(4, HD, 2 * HD)
+        return carry
+
+    lax.fori_loop(0, PIECES, project, 0)
+
+    for j in range(4):
+        s_copy(j).start()
+    for j in range(4):
+        s_copy(j).wait_recv()
+        total = sums[side, j] + partner_sums[j]
+        key_rows = jnp.concatenate([total[:, :64], total[:, 128:192]], axis=1)
+        value_rows = jnp.concatenate([total[:, 64:128], total[:, 192:]], axis=1)
+        frame = frame_at(z1, j, x)
+        kv[frame, 0] = key_rows.T.astype(jnp.bfloat16)
+        kv[frame, 1] = value_rows.astype(jnp.bfloat16)
+        kv_copy(1, j).start()
+        kv_copy(0, j).start()
+    for j in range(4):
+        kv_arrival(1, j).wait_recv()
+        kv_copy(2, j).start()
+    for t in (1, 2, 3):
+        l_arrival(t).wait_recv()
+        q_arrival(t).wait_recv()
+    for j in range(4):
+        kv_arrival(0, j).wait_recv()
+        kv_arrival(2, j).wait_recv()
+
+    frames = kv.shape[0]
+    keys = frames * HD
+    gate = jnp.tanh(jnp.full((1, HD), gate_ref[0], jnp.float32))
+    factor = HD ** (-0.5) * 1.4426950408889634
+
+    for t in (1, 2, 3, 0):
+        last_rows = jnp.broadcast_to(last_all[peer(t), 0:1, :], (HD, HD)).T
+        for frame in range(frames):
+            bias[:, frame * HD:(frame + 1) * HD] = jnp.where(
+                last_rows >= frame, 0.0, -1e30
+            ).astype(jnp.float32)
+
+        def heads(step, carry, t=t):
+            start = pl.multiple_of(step * STACK * HD, STACK * HD)
+            pair = q_all[peer(t), :, pl.ds(start, STACK * HD)]
+            stacked = jnp.concatenate([pair[:, i * HD:(i + 1) * HD] for i in range(STACK)], axis=0)
+            key_columns = jnp.concatenate([kv[frame, 0] for frame in range(frames)], axis=1)
+            scores = jnp.dot(stacked, key_columns, preferred_element_type=jnp.float32)
+            scores = (scores.reshape(STACK, HD, keys) + bias[...][None]).reshape(STACK * HD, keys)
+            row_max = jnp.max(scores, axis=1, keepdims=True)
+            exps = jnp.exp2((scores - row_max) * factor)
+            denominator = jnp.sum(exps, axis=1, keepdims=True)
+            value_rows = kv[:, 1].reshape(keys, HD)
+            numerator = jnp.dot(
+                exps.astype(jnp.bfloat16), value_rows, preferred_element_type=jnp.float32
+            )
+            result = (gate * (numerator / denominator)).astype(jnp.bfloat16)
+            out_parts[t, :, pl.ds(start, STACK * HD)] = jnp.concatenate(
+                [result[i * HD:(i + 1) * HD] for i in range(STACK)], axis=1
+            )
+            return carry
+
+        lax.fori_loop(0, width // (STACK * HD), heads, 0)
+        if t:
+            o_copy(t).start()
+    out_ref[:, columns_of(member)] = out_parts[0]
+
+    def sent(k, carry):
+        for kind in range(3):
+            w_copy(kind, k).wait_send()
+            c_copy(kind, k).wait_send()
+        return carry
+
+    lax.fori_loop(0, PIECES, sent, 0)
+    for j in range(4):
+        s_copy(j).wait_send()
+        for kind in range(3):
+            kv_copy(kind, j).wait_send()
+    for t in (1, 2, 3):
+        l_copy(t).wait_send()
+        q_copy(t).wait_send()
+        o_copy(t).wait_send()
+        o_arrival(t).wait_recv()
+
+
+def fused_local(vision, kept_index, w_key, w_value, queries, last_frame, attn_gate):
+    patches, features = vision.shape[1:]
+    rows, row_width = queries.shape
+    width = row_width // 4
+    depth = features // PIECES
+    main_rows = (patches - 1) // HD * HD
+    tail = vision[0, patches - HD:]
+    vmem = pl.BlockSpec(memory_space=pltpu.VMEM)
+    dma = pltpu.SemaphoreType.DMA
+    return pl.pallas_call(
+        fused_kernel,
+        out_shape=jax.ShapeDtypeStruct(queries.shape, jnp.bfloat16),
+        in_specs=[pl.BlockSpec(memory_space=pl.ANY)] + [vmem] * 6
+        + [pl.BlockSpec(memory_space=pltpu.SMEM)],
+        out_specs=vmem,
+        scratch_shapes=[
+            pltpu.VMEM((2, main_rows, depth), jnp.bfloat16),
+            pltpu.VMEM((HD, main_rows + HD), jnp.bfloat16),
+            pltpu.VMEM((PIECES, 4, HD, depth), jnp.bfloat16),
+            pltpu.VMEM((PIECES, 2, 2, depth, HD), jnp.bfloat16),
+            pltpu.VMEM((2, 4, HD, 2 * HD), jnp.float32),
+            pltpu.VMEM((4, HD, 2 * HD), jnp.float32),
+            pltpu.VMEM((16, 2, HD, HD), jnp.bfloat16),
+            pltpu.VMEM((4, rows, width), jnp.bfloat16),
+            pltpu.VMEM((4, 8, HD), jnp.int32),
+            pltpu.VMEM((rows, 16 * HD), jnp.float32),
+            pltpu.VMEM((4, rows, width), jnp.bfloat16),
+            dma((2,)),
+            dma((3, PIECES)), dma((3, PIECES)),
+            dma((3, PIECES)), dma((3, PIECES)),
+            dma((4,)), dma((4,)), dma((4,)), dma((4,)), dma((4,)), dma((4,)),
+            dma((3, 4)), dma((3, 4)),
+            dma((4,)), dma((4,)),
+        ],
+        compiler_params=pltpu.CompilerParams(
+            collective_id=0, has_side_effects=True, vmem_limit_bytes=52 * 2**20
+        ),
+    )(vision, tail, kept_index, w_key, w_value, queries, last_frame.reshape(1, rows), attn_gate)
 
 
 def fold_frames(running, query_heads, last_rows, key_piece, value_piece):
@@ -87,4 +389,8 @@
         P(),
     )
     out_specs = P("blk", "head")
+    if dict(mesh.shape) == {"blk": 16, "head": 2}:
+        return jax.shard_map(
+            fused_local, mesh=mesh, in_specs=in_specs, out_specs=out_specs, check_vma=False
+        )
     return jax.shard_map(local, mesh=mesh, in_specs=in_specs, out_specs=out_specs, check_vma=False)

time: 368 us -> 117 us (0.32)
  waiting for transfers between devices: 280 us -> 0 us
  Pallas kernels: 0 us -> 107 us
  matrix products: 30.8 us -> 0 us
  other arithmetic: 24 us -> 0 us
  between operations: 13.9 us -> 0.66 us
  local copies, waits for them, and re-layouts: 17.9 us -> 9.54 us
    all_gather x3 -> x0, waiting for transfers between devices: 273 us -> none  [the longest x1 186 us: local(): lax.all_gather(stacked, 'blk', axis=2, tiled=True)]
    pallas_call x0 -> x1, Pallas kernels: none -> 107 us  [fused_local(): pl.pallas_call(fused_kernel, out_shape=jax.ShapeDtypeStruct(queries.shape...]
    dot_general x3 -> x0, matrix products: 30.8 us -> none  [the longest x1 13.5 us: fold_frames(): jnp.einsum('rkgd,fjkd->rkgfj', query_heads, key_piece, preferred_element_...]
    convert_element_type x2 -> x0, other arithmetic: 21.1 us -> none  [the longest x1 20 us: fold_frames(): weights = exps.astype(jnp.bfloat16)]
    gather x1 -> x0, local copies, waits for them, and re-layouts: 8.73 us -> none  [local(): chosen = vision[0][kept_index[0]]]
    reduce_scatter x1 -> x0, waiting for transfers between devices: 6.85 us -> none  [local(): lax.psum_scatter(partial_value, 'head', scatter_dimension=2, tiled=True)]
    unnamed x5 -> x7, local copies, waits for them, and re-layouts: 0.25 us -> 7.06 us
    all_gather x2 -> x0, local copies, waits for them, and re-layouts: 6.06 us -> none  [the longest x1 3.03 us: attend(): key_piece = lax.all_gather(key_rows, 'blk', axis=0, tiled=True)]
  transfers between devices with their start and end apart: 4 -> 0, of which waited for: 4 -> 0; matrix products, arithmetic and copies ran while one was open for 13% -> 0% of each run, Pallas kernels for 0% -> 0%
where the time goes in v1:
time: 117 us
  Pallas kernels  107 us (91%)
  local copies, waits for them, and re-layouts  9.54 us (8%)
    pallas_call x1, Pallas kernels, fused_local(): pl.pallas_call(fused_kernel, out_shape=jax.ShapeDtypeStruct(queries.shape...  107 us
    unnamed x7, local copies, waits for them, and re-layouts  7.06 us
    squeeze x1, local copies, waits for them, and re-layouts, fused_local(): tail = vision[0, patches - HD:]  2.48 us

profile of v1, /device:TPU:0, one launch (start us, length us, event | category | flops | bytes accessed | tf_op | source)
XLA Modules:
  0.0 117.0 jit_solution(17593533386987335678)
XLA Ops:
  0.7 2.4 %copy.8.w_key_ref = bf16[4096,64]{1,0:T(8,128)(2,1)} copy(bf16[4096,64]{0,1:T(8,128)(2,1)} %param.9) | data formatting | bytes 1048576 | tf_op args[2]
  3.0 2.4 %copy.9.w_value_ref = bf16[4096,64]{1,0:T(8,128)(2,1)} copy(bf16[4096,64]{0,1:T(8,128)(2,1)} %param.10) | data formatting | bytes 1048576 | tf_op args[3]
  5.4 2.5 %slice_bitcast_fusion.tail_ref = bf16[128,4096]{1,0:T(8,128)(2,1)} fusion(bf16[1,1601,4096]{2,1,0:T(8,128)(2,1)} %vision_ref.1), kind=kLoop, calls=%fused_computation | loop fusion | bytes 2097152 | tf_op jit(solution)/shard_map/squeeze | solution.py:277
  7.9 0.0 copy-start
  7.9 0.7 copy-done
  8.6 0.0 copy-start.1
  8.6 0.7 copy-done.1
  9.2 106.8 %shard_map.73 = bf16[128,4096]{1,0:T(8,128)(2,1)S(1)} custom-call(bf16[1,1601,4096]{2,1,0:T(8,128)(2,1)} %vision_ref.1, bf16[128,4096]{1,0:T(8,128)(2,1)} %slice_bitcast_fusion.tail_ref, s32[1,128]{1,0:T(1,128)S(1)} %copy-done, bf16[4096,64]{1,0:T(8,128)(2,1)} %copy.8.w_key_ref, bf16[4096,64]{1,0:T(8,128)(2,1)} %copy.9.w_value_ref, bf16[128,4096]{1,0:T(8,128)(2,1)} %q_ref.1, ...), custom_call_target="tpu_custom_call" | custom-call | tf_op jit(solution)/shard_map/pallas_call | solution.py:280
  116.0 1.0 copy.12
Async XLA Ops:
  7.9 0.7 copy-start
  8.6 0.7 copy-start.1

commit v2 on v1

--- a/solution.py
+++ b/solution.py
@@ -12,10 +12,12 @@
 
 
 def fused_kernel(
-    vision_ref, tail_ref, index_ref, w_key_ref, w_value_ref, q_ref, last_ref, gate_ref, out_ref,
-    vision_buf, onehot, chosen, weights, sums, partner_sums, kv, q_all, last_all, bias, out_parts,
-    vision_sem, w_send, w_recv, c_send, c_recv, q_send, q_recv, l_send, l_recv,
-    s_send, s_recv, kv_send, kv_recv, o_send, o_recv,
+    vision_ref, index_hbm, w_key_ref, w_value_ref, q_ref, last_hbm, gate_ref, out_ref,
+    vision_buf, index_ref, last_ref, onehot, chosen, weights, sums, partner_sums, keys_all,
+    values_all, q_all, last_all, exps_own, exps_even, exps_odd, dens_own, dens_even, dens_odd,
+    out_parts, vision_sem, small_sem, load_sem,
+    w_send, w_recv, c_send, c_recv, q_send, q_recv, l_send, l_recv,
+    s_send, s_recv, k_send, k_recv, v_send, v_recv, o_send, o_recv,
 ):
     blk = lax.axis_index("blk")
     side = lax.axis_index("head")
@@ -37,13 +39,13 @@
         )
 
     depth = chosen.shape[3]
-    main_rows = vision_buf.shape[1]
+    patches = vision_buf.shape[1]
 
     def vision_copy(k):
         columns = pl.ds(pl.multiple_of(k * depth, depth), depth)
         slot = lax.rem(k, 2)
         return pltpu.make_async_copy(
-            vision_ref.at[0, pl.ds(0, main_rows), columns], vision_buf.at[slot], vision_sem.at[slot]
+            vision_ref.at[0, :, columns], vision_buf.at[slot], vision_sem.at[slot]
         )
 
     def w_copy(kind, k):
@@ -64,13 +66,16 @@
         slot = chosen.at[k, from_z0 * 2 + from_y]
         return send(slot, slot, c_send.at[kind, k], c_recv.at[kind, k], to_y)
 
-    def kv_copy(kind, j):
-        slot = kv.at[frame_at(z1 if kind < 2 else 1 - z1, j, x)]
-        return send(slot, slot, kv_send.at[kind, j], kv_recv.at[kind, j], to_z1 if kind == 1 else to_x)
-
-    def kv_arrival(kind, j):
-        slot = kv.at[frame_at(z1 if kind == 0 else 1 - z1, j, x if kind == 1 else 1 - x)]
-        return send(slot, slot, kv_send.at[kind, j], kv_recv.at[kind, j], to_x)
+    def kv_copy(held, send_sem, recv_sem, kind, j):
+        slot = held.at[frame_at(z1 if kind < 2 else 1 - z1, j, x)]
+        return send(slot, slot, send_sem.at[kind, j], recv_sem.at[kind, j], to_z1 if kind == 1 else to_x)
+
+    def kv_arrival(held, send_sem, recv_sem, kind, j):
+        slot = held.at[frame_at(z1 if kind == 0 else 1 - z1, j, x if kind == 1 else 1 - x)]
+        return send(slot, slot, send_sem.at[kind, j], recv_sem.at[kind, j], to_x)
+
+    key_part = (keys_all, k_send, k_recv)
+    value_part = (values_all, v_send, v_recv)
 
     width = q_all.shape[2]
 
@@ -107,47 +112,57 @@
     def s_copy(j):
         return send(sums.at[1 - side, j], partner_sums.at[j], s_send.at[j], s_recv.at[j], to_core)
 
-    vision_copy(0).start()
-    vision_copy(1).start()
-
-    def join_weights(k, carry):
-        rows = pl.ds(pl.multiple_of(k * depth, depth), depth)
-        weights[k, z1, x] = jnp.concatenate([w_key_ref[rows, :], w_value_ref[rows, :]], axis=1)
-        return carry
-
-    lax.fori_loop(0, PIECES, join_weights, 0)
+    def w_load(which, k):
+        columns = pl.ds(pl.multiple_of(k * depth, depth), depth)
+        return pltpu.make_async_copy(
+            (w_key_ref, w_value_ref)[which].at[:, columns],
+            weights.at[k, z1, x, pl.ds(which * 64, 64)], load_sem.at[which, k],
+        )
+
+    own_q = pltpu.make_async_copy(q_ref.at[:, columns_of(member)], q_all.at[member], small_sem.at[0])
+    index_copy = pltpu.make_async_copy(index_hbm, index_ref, small_sem.at[1])
+    last_copy = pltpu.make_async_copy(last_hbm, last_ref, small_sem.at[2])
 
     barrier = pltpu.get_barrier_semaphore()
     for device in partners:
         pl.semaphore_signal(barrier, inc=1, device_id=device, device_id_type=MESH)
+
+    def load_weights(k, carry):
+        w_load(0, k).start()
+        w_load(1, k).start()
+        return carry
+
+    index_copy.start()
+    last_copy.start()
+    lax.fori_loop(0, PIECES, load_weights, 0)
+    vision_copy(0).start()
+    vision_copy(1).start()
+    own_q.start()
     pl.semaphore_wait(barrier, len(partners))
 
     def send_weights(k, carry):
+        w_load(0, k).wait()
+        w_load(1, k).wait()
         w_copy(1, k).start()
         w_copy(0, k).start()
         return carry
 
     lax.fori_loop(0, PIECES, send_weights, 0)
 
+    index_copy.wait()
+    last_copy.wait()
     index_rows = jnp.broadcast_to(index_ref[...], (HD, HD)).T
     lanes = lax.broadcasted_iota(jnp.int32, (HD, HD), 1)
-    for block in range(main_rows // HD):
-        onehot[:, block * HD:(block + 1) * HD] = jnp.where(
-            index_rows == lanes + block * HD, 1.0, 0.0
-        ).astype(jnp.bfloat16)
-    tail_start = vision_ref.shape[1] - HD
-    tail_rows = lanes + tail_start
-    onehot[:, main_rows:] = jnp.where(
-        (index_rows == tail_rows) & (tail_rows >= main_rows), 1.0, 0.0
-    ).astype(jnp.bfloat16)
+    for start in range(0, patches, HD):
+        stop = min(start + HD, patches)
+        onehot[:, start:stop] = jnp.where(index_rows == lanes + start, 1.0, 0.0).astype(
+            jnp.bfloat16
+        )[:, :stop - start]
 
     def choose(k, carry):
         vision_copy(k).wait()
-        columns = pl.ds(pl.multiple_of(k * depth, depth), depth)
         picked = jnp.dot(
-            onehot[:, :main_rows], vision_buf[lax.rem(k, 2)], preferred_element_type=jnp.float32
-        ) + jnp.dot(
-            onehot[:, main_rows:], tail_ref[:, columns], preferred_element_type=jnp.float32
+            onehot[...], vision_buf[lax.rem(k, 2)], preferred_element_type=jnp.float32
         )
         chosen[k, member] = picked.astype(jnp.bfloat16)
         c_copy(1, k).start()
@@ -160,12 +175,6 @@
         return carry
 
     lax.fori_loop(0, PIECES, choose, 0)
-
-    last_all[member] = jnp.broadcast_to(last_ref[...], (8, HD))
-    q_all[member] = q_ref[:, columns_of(member)]
-    for t in (1, 2, 3):
-        l_copy(t).start()
-        q_copy(t).start()
 
     def relay(k, carry):
         w_arrival(1, k).wait_recv()
@@ -175,6 +184,11 @@
         return carry
 
     lax.fori_loop(0, PIECES, relay, 0)
+
+    last_all[member] = jnp.broadcast_to(last_ref[...], (8, HD))
+    for t in (1, 2, 3):
+        l_copy(t).start()
+        q_copy(t).start()
 
     sums[...] = jnp.zeros_like(sums)
 
@@ -184,8 +198,10 @@
             c_arrival(kind, k).wait_recv()
         rows = chosen[k].reshape(4 * HD, depth)
         for group in range(2):
-            columns = jnp.concatenate([weights[k, group, 0], weights[k, group, 1]], axis=1)
-            added = jnp.dot(rows, columns, preferred_element_type=jnp.float32)
+            columns = weights[k, group].reshape(2 * HD, depth)
+            added = lax.dot_general(
+                rows, columns, (((1,), (1,)), ((), ())), preferred_element_type=jnp.float32
+            )
             sums[group] += added.reshape(4, HD, 2 * HD)
         return carry
 
@@ -199,55 +215,90 @@
         key_rows = jnp.concatenate([total[:, :64], total[:, 128:192]], axis=1)
         value_rows = jnp.concatenate([total[:, 64:128], total[:, 192:]], axis=1)
         frame = frame_at(z1, j, x)
-        kv[frame, 0] = key_rows.T.astype(jnp.bfloat16)
-        kv[frame, 1] = value_rows.astype(jnp.bfloat16)
-        kv_copy(1, j).start()
-        kv_copy(0, j).start()
-    for j in range(4):
-        kv_arrival(1, j).wait_recv()
-        kv_copy(2, j).start()
+        keys_all[frame] = key_rows.T.astype(jnp.bfloat16)
+        values_all[frame] = value_rows.astype(jnp.bfloat16)
+        kv_copy(*key_part, 1, j).start()
+        kv_copy(*key_part, 0, j).start()
+    for j in range(4):
+        kv_copy(*value_part, 1, j).start()
+        kv_copy(*value_part, 0, j).start()
+    for part in (key_part, value_part):
+        for j in range(4):
+            kv_arrival(*part, 1, j).wait_recv()
+            kv_copy(*part, 2, j).start()
+    own_q.wait()
+    for j in range(4):
+        kv_arrival(*key_part, 0, j).wait_recv()
+        kv_arrival(*key_part, 2, j).wait_recv()
+
+    frames = keys_all.shape[0]
+    keys = frames * HD
+    gate = jnp.tanh(jnp.full((1, HD), gate_ref[0], jnp.float32))
+    factor = HD ** (-0.5) * 1.4426950408889634
+    steps = width // (STACK * HD)
+    feature = lax.broadcasted_iota(jnp.int32, (HD, HD), 0)
+
+    def hidden_of(t):
+        last_rows = jnp.broadcast_to(last_all[peer(t), 0:1, :], (HD, HD)).T
+        hidden = jnp.where(last_rows < lanes, -1e30, 0.0).astype(jnp.bfloat16)
+        return jnp.concatenate([hidden] * STACK, axis=0)
+
+    def weigh(t, hidden, step, exps_ref, dens_ref):
+        start = pl.multiple_of(step * STACK * HD, STACK * HD)
+        heads = q_all[peer(t), :, pl.ds(start, STACK * HD)]
+        stacked = jnp.concatenate([heads[:, i * HD:(i + 1) * HD] for i in range(STACK)], axis=0)
+        key_columns = jnp.concatenate([keys_all[frame] for frame in range(frames)], axis=1)
+        marks = jnp.concatenate(
+            [jnp.where(feature == frame, 1.0, 0.0).astype(jnp.bfloat16) for frame in range(frames)],
+            axis=1,
+        )
+        scores = jnp.dot(
+            jnp.concatenate([stacked, hidden], axis=1),
+            jnp.concatenate([key_columns, marks], axis=0),
+            preferred_element_type=jnp.float32,
+        )
+        row_max = jnp.max(scores, axis=1, keepdims=True)
+        exps = jnp.exp2((scores - row_max) * factor)
+        dens_ref[step] = jnp.broadcast_to(jnp.sum(exps, axis=1, keepdims=True), (STACK * HD, HD))
+        exps_ref[step] = exps.astype(jnp.bfloat16)
+
+    def combine(t, step, exps_ref, dens_ref):
+        start = pl.multiple_of(step * STACK * HD, STACK * HD)
+        value_rows = values_all[...].reshape(keys, HD)
+        numerator = jnp.dot(exps_ref[step], value_rows, preferred_element_type=jnp.float32)
+        result = (gate * (numerator / dens_ref[step])).astype(jnp.bfloat16)
+        out_parts[t, :, pl.ds(start, STACK * HD)] = jnp.concatenate(
+            [result[i * HD:(i + 1) * HD] for i in range(STACK)], axis=1
+        )
+
+    def run(weighed, combined):
+        hidden = hidden_of(weighed[0]) if weighed else None
+
+        def body(step, carry):
+            if combined:
+                combine(combined[0], step, *combined[1])
+            if weighed:
+                weigh(weighed[0], hidden, step, *weighed[1])
+            return carry
+
+        lax.fori_loop(0, steps, body, 0)
+
+    own, even, odd = (exps_own, dens_own), (exps_even, dens_even), (exps_odd, dens_odd)
+    run((0, own), None)
     for t in (1, 2, 3):
         l_arrival(t).wait_recv()
         q_arrival(t).wait_recv()
-    for j in range(4):
-        kv_arrival(0, j).wait_recv()
-        kv_arrival(2, j).wait_recv()
-
-    frames = kv.shape[0]
-    keys = frames * HD
-    gate = jnp.tanh(jnp.full((1, HD), gate_ref[0], jnp.float32))
-    factor = HD ** (-0.5) * 1.4426950408889634
-
-    for t in (1, 2, 3, 0):
-        last_rows = jnp.broadcast_to(last_all[peer(t), 0:1, :], (HD, HD)).T
-        for frame in range(frames):
-            bias[:, frame * HD:(frame + 1) * HD] = jnp.where(
-                last_rows >= frame, 0.0, -1e30
-            ).astype(jnp.float32)
-
-        def heads(step, carry, t=t):
-            start = pl.multiple_of(step * STACK * HD, STACK * HD)
-            pair = q_all[peer(t), :, pl.ds(start, STACK * HD)]
-            stacked = jnp.concatenate([pair[:, i * HD:(i + 1) * HD] for i in range(STACK)], axis=0)
-            key_columns = jnp.concatenate([kv[frame, 0] for frame in range(frames)], axis=1)
-            scores = jnp.dot(stacked, key_columns, preferred_element_type=jnp.float32)
-            scores = (scores.reshape(STACK, HD, keys) + bias[...][None]).reshape(STACK * HD, keys)
-            row_max = jnp.max(scores, axis=1, keepdims=True)
-            exps = jnp.exp2((scores - row_max) * factor)
-            denominator = jnp.sum(exps, axis=1, keepdims=True)
-            value_rows = kv[:, 1].reshape(keys, HD)
-            numerator = jnp.dot(
-                exps.astype(jnp.bfloat16), value_rows, preferred_element_type=jnp.float32
-            )
-            result = (gate * (numerator / denominator)).astype(jnp.bfloat16)
-            out_parts[t, :, pl.ds(start, STACK * HD)] = jnp.concatenate(
-                [result[i * HD:(i + 1) * HD] for i in range(STACK)], axis=1
-            )
-            return carry
-
-        lax.fori_loop(0, width // (STACK * HD), heads, 0)
-        if t:
-            o_copy(t).start()
+    run((2, even), None)
+    for j in range(4):
+        kv_arrival(*value_part, 0, j).wait_recv()
+        kv_arrival(*value_part, 2, j).wait_recv()
+    run((1, odd), (2, even))
+    o_copy(2).start()
+    run((3, even), (1, odd))
+    o_copy(1).start()
+    run(None, (3, even))
+    o_copy(3).start()
+    run(None, (0, own))
     out_ref[:, columns_of(member)] = out_parts[0]
 
     def sent(k, carry):
@@ -260,7 +311,8 @@
     for j in range(4):
         s_copy(j).wait_send()
         for kind in range(3):
-            kv_copy(kind, j).wait_send()
+            kv_copy(*key_part, kind, j).wait_send()
+            kv_copy(*value_part, kind, j).wait_send()
     for t in (1, 2, 3):
         l_copy(t).wait_send()
         q_copy(t).wait_send()
@@ -273,39 +325,42 @@
     rows, row_width = queries.shape
     width = row_width // 4
     depth = features // PIECES
-    main_rows = (patches - 1) // HD * HD
-    tail = vision[0, patches - HD:]
-    vmem = pl.BlockSpec(memory_space=pltpu.VMEM)
+    steps = width // (STACK * HD)
+    vmem = pltpu.VMEM
     dma = pltpu.SemaphoreType.DMA
+    exps = vmem((steps, STACK * HD, 16 * HD), jnp.bfloat16)
+    dens = vmem((steps, STACK * HD, HD), jnp.float32)
     return pl.pallas_call(
         fused_kernel,
         out_shape=jax.ShapeDtypeStruct(queries.shape, jnp.bfloat16),
-        in_specs=[pl.BlockSpec(memory_space=pl.ANY)] + [vmem] * 6
-        + [pl.BlockSpec(memory_space=pltpu.SMEM)],
-        out_specs=vmem,
+        in_specs=[pl.BlockSpec(memory_space=pl.ANY)] * 6 + [pl.BlockSpec(memory_space=pltpu.SMEM)],
+        out_specs=pl.BlockSpec(memory_space=vmem),
         scratch_shapes=[
-            pltpu.VMEM((2, main_rows, depth), jnp.bfloat16),
-            pltpu.VMEM((HD, main_rows + HD), jnp.bfloat16),
-            pltpu.VMEM((PIECES, 4, HD, depth), jnp.bfloat16),
-            pltpu.VMEM((PIECES, 2, 2, depth, HD), jnp.bfloat16),
-            pltpu.VMEM((2, 4, HD, 2 * HD), jnp.float32),
-            pltpu.VMEM((4, HD, 2 * HD), jnp.float32),
-            pltpu.VMEM((16, 2, HD, HD), jnp.bfloat16),
-            pltpu.VMEM((4, rows, width), jnp.bfloat16),
-            pltpu.VMEM((4, 8, HD), jnp.int32),
-            pltpu.VMEM((rows, 16 * HD), jnp.float32),
-            pltpu.VMEM((4, rows, width), jnp.bfloat16),
-            dma((2,)),
+            vmem((2, patches, depth), jnp.bfloat16),
+            vmem((1, HD), jnp.int32),
+            vmem((1, rows), jnp.int32),
+            vmem((HD, patches), jnp.bfloat16),
+            vmem((PIECES, 4, HD, depth), jnp.bfloat16),
+            vmem((PIECES, 2, 2, HD, depth), jnp.bfloat16),
+            vmem((2, 4, HD, 2 * HD), jnp.float32),
+            vmem((4, HD, 2 * HD), jnp.float32),
+            vmem((16, HD, HD), jnp.bfloat16),
+            vmem((16, HD, HD), jnp.bfloat16),
+            vmem((4, rows, width), jnp.bfloat16),
+            vmem((4, 8, HD), jnp.int32),
+            exps, exps, exps, dens, dens, dens,
+            vmem((4, rows, width), jnp.bfloat16),
+            dma((2,)), dma((3,)), dma((2, PIECES)),
             dma((3, PIECES)), dma((3, PIECES)),
             dma((3, PIECES)), dma((3, PIECES)),
             dma((4,)), dma((4,)), dma((4,)), dma((4,)), dma((4,)), dma((4,)),
-            dma((3, 4)), dma((3, 4)),
+            dma((3, 4)), dma((3, 4)), dma((3, 4)), dma((3, 4)),
             dma((4,)), dma((4,)),
         ],
         compiler_params=pltpu.CompilerParams(
-            collective_id=0, has_side_effects=True, vmem_limit_bytes=52 * 2**20
+            collective_id=0, has_side_effects=True, vmem_limit_bytes=56 * 2**20
         ),
-    )(vision, tail, kept_index, w_key, w_value, queries, last_frame.reshape(1, rows), attn_gate)
+    )(vision, kept_index, w_key.T, w_value.T, queries, last_frame.reshape(1, rows), attn_gate)
 
 
 def fold_frames(running, query_heads, last_rows, key_piece, value_piece):

time: 117 us -> 111 us (0.949)
  local copies, waits for them, and re-layouts: 9.54 us -> 2.29 us
    unnamed x7 -> x1, local copies, waits for them, and re-layouts: 7.06 us -> 2.29 us
    squeeze x1 -> x0, local copies, waits for them, and re-layouts: 2.48 us -> none  [fused_local(): tail = vision[0, patches - HD:]]
where the time goes in v2:
time: 111 us
  Pallas kernels  108 us (97%)
  local copies, waits for them, and re-layouts  2.29 us (2%)
    pallas_call x1, Pallas kernels, fused_local(): pl.pallas_call(fused_kernel, out_shape=jax.ShapeDtypeStruct(queries.shape...  108 us
    unnamed x1, local copies, waits for them, and re-layouts  2.29 us

profile of v2, /device:TPU:0, one launch (start us, length us, event | category | flops | bytes accessed | tf_op | source)
XLA Modules:
  0.0 110.7 jit_solution(15802570213143993751)
XLA Ops:
  0.7 107.7 %shard_map.73 = bf16[128,4096]{1,0:T(8,128)(2,1)} custom-call(bf16[1,1601,4096]{2,1,0:T(8,128)(2,1)} %vision_ref.1, s32[1,128]{1,0:T(1,128)} %index_hbm.1, bf16[64,4096]{1,0:T(8,128)(2,1)} %bitcast.3, bf16[64,4096]{1,0:T(8,128)(2,1)} %bitcast.4, bf16[128,4096]{1,0:T(8,128)(2,1)} %q_ref.1, s32[1,128]{1,0:T(1,128)} %bitcast.5, f32[1]{0:T(128)S(6)} %copy.9.gate_ref), custom_call_target="tpu_custom_call" | custom-call | tf_op jit(solution)/shard_map/pallas_call | solution.py:333
  108.4 2.3 %copy.10 = bf16[128,4096]{1,0:T(8,128)(2,1)} copy(bf16[128,4096]{1,0:T(8,128)(2,1)} %shard_map.73) | data formatting | bytes 2097152

commit v3 on v2

--- a/solution.py
+++ b/solution.py
@@ -8,6 +8,7 @@
 HD = 128
 MESH = pl.DeviceIdType.MESH
 PIECES = 8
+LAG = 3
 STACK = 2
 
 
@@ -176,23 +177,10 @@
 
     lax.fori_loop(0, PIECES, choose, 0)
 
-    def relay(k, carry):
-        w_arrival(1, k).wait_recv()
-        w_copy(2, k).start()
-        c_arrival(1, k).wait_recv()
-        c_copy(2, k).start()
-        return carry
-
-    lax.fori_loop(0, PIECES, relay, 0)
-
     last_all[member] = jnp.broadcast_to(last_ref[...], (8, HD))
-    for t in (1, 2, 3):
-        l_copy(t).start()
-        q_copy(t).start()
-
     sums[...] = jnp.zeros_like(sums)
 
-    def project(k, carry):
+    def project(k):
         for kind in (0, 2):
             w_arrival(kind, k).wait_recv()
             c_arrival(kind, k).wait_recv()
@@ -203,9 +191,28 @@
                 rows, columns, (((1,), (1,)), ((), ())), preferred_element_type=jnp.float32
             )
             sums[group] += added.reshape(4, HD, 2 * HD)
+
+    def relay_and_project(k, carry):
+        @pl.when(k < PIECES)
+        def _():
+            w_arrival(1, k).wait_recv()
+            w_copy(2, k).start()
+            c_arrival(1, k).wait_recv()
+            c_copy(2, k).start()
+
+        @pl.when(k == PIECES - 1)
+        def _():
+            for t in (1, 2, 3):
+                l_copy(t).start()
+                q_copy(t).start()
+
+        @pl.when(k >= LAG)
+        def _():
+            project(k - LAG)
+
         return carry
 
-    lax.fori_loop(0, PIECES, project, 0)
+    lax.fori_loop(0, PIECES + LAG, relay_and_project, 0)
 
     for j in range(4):
         s_copy(j).start()
@@ -221,11 +228,14 @@
         kv_copy(*key_part, 0, j).start()
     for j in range(4):
         kv_copy(*value_part, 1, j).start()
+    for j in range(4):
+        kv_arrival(*key_part, 1, j).wait_recv()
+        kv_copy(*key_part, 2, j).start()
+    for j in range(4):
         kv_copy(*value_part, 0, j).start()
-    for part in (key_part, value_part):
-        for j in range(4):
-            kv_arrival(*part, 1, j).wait_recv()
-            kv_copy(*part, 2, j).start()
+    for j in range(4):
+        kv_arrival(*value_part, 1, j).wait_recv()
+        kv_copy(*value_part, 2, j).start()
     own_q.wait()
     for j in range(4):
         kv_arrival(*key_part, 0, j).wait_recv()
@@ -333,7 +343,7 @@
     return pl.pallas_call(
         fused_kernel,
         out_shape=jax.ShapeDtypeStruct(queries.shape, jnp.bfloat16),
-        in_specs=[pl.BlockSpec(memory_space=pl.ANY)] * 6 + [pl.BlockSpec(memory_space=pltpu.SMEM)],
+        in_specs=[pl.BlockSpec(memory_space=pltpu.HBM)] * 6 + [pl.BlockSpec(memory_space=pltpu.SMEM)],
         out_specs=pl.BlockSpec(memory_space=vmem),
         scratch_shapes=[
             vmem((2, patches, depth), jnp.bfloat16),
@@ -358,7 +368,7 @@
             dma((4,)), dma((4,)),
         ],
         compiler_params=pltpu.CompilerParams(
-            collective_id=0, has_side_effects=True, vmem_limit_bytes=56 * 2**20
+            collective_id=0, has_side_effects=True, vmem_limit_bytes=46 * 2**20
         ),
     )(vision, kept_index, w_key.T, w_value.T, queries, last_frame.reshape(1, rows), attn_gate)
 

time: 111 us -> 111 us (level)
  local copies, waits for them, and re-layouts: 2.29 us -> 5.58 us
  Pallas kernels: 108 us -> 105 us
    unnamed x1 -> x11, local copies, waits for them, and re-layouts: 2.29 us -> 5.58 us
    pallas_call x1, Pallas kernels: 108 us -> 105 us  [fused_local(): pl.pallas_call(fused_kernel, out_shape=jax.ShapeDtypeStruct(queries.shape...]
where the time goes in v3:
time: 111 us
  Pallas kernels  105 us (95%)
  local copies, waits for them, and re-layouts  5.58 us (5%)
    pallas_call x1, Pallas kernels, fused_local(): pl.pallas_call(fused_kernel, out_shape=jax.ShapeDtypeStruct(queries.shape...  105 us
    unnamed x11, local copies, waits for them, and re-layouts  5.58 us

profile of v3, /device:TPU:0, one launch (start us, length us, event | category | flops | bytes accessed | tf_op | source)
XLA Modules:
  0.0 110.9 jit_solution(17423258312226678130)
XLA Ops:
  0.7 0.0 copy-start
  0.7 1.2 %copy-done = bf16[128,4096]{1,0:T(8,128)(2,1)S(1)} copy-done((bf16[128,4096]{1,0:T(8,128)(2,1)S(1)}, bf16[128,4096]{1,0:T(8,128)(2,1)}, u32[]{:S(2)}) %copy-start) | copy-done | bytes 1048600
  1.9 0.0 copy-start.1
  1.9 1.0 copy-done.1
  2.9 0.0 copy-start.2
  2.9 1.0 copy-done.2
  4.0 0.0 copy-start.3
  4.0 0.7 copy-done.3
  4.6 0.0 copy-start.4
  4.6 0.7 copy-done.4
  5.3 104.6 %shard_map.73 = bf16[128,4096]{1,0:T(8,128)(2,1)S(1)} custom-call(bf16[1,1601,4096]{2,1,0:T(8,128)(2,1)} %vision_ref.1, s32[1,128]{1,0:T(1,128)S(1)} %copy-done.3, bf16[64,4096]{1,0:T(8,128)(2,1)S(1)} %bitcast.3, bf16[64,4096]{1,0:T(8,128)(2,1)S(1)} %bitcast.4, bf16[128,4096]{1,0:T(8,128)(2,1)S(1)} %copy-done, s32[1,128]{1,0:T(1,128)S(1)} %bitcast.5, ...), custom_call_target="tpu_custom_call" | custom-call | tf_op jit(solution)/shard_map/pallas_call | solution.py:343
  109.9 1.0 copy.10
Async XLA Ops:
  0.7 1.2 %copy-start = (bf16[128,4096]{1,0:T(8,128)(2,1)S(1)}, bf16[128,4096]{1,0:T(8,128)(2,1)}, u32[]{:S(2)}) copy-start(bf16[128,4096]{1,0:T(8,128)(2,1)} %q_ref.1) | copy-start | bytes 3145732
  1.9 1.0 copy-start.1
  2.9 1.0 copy-start.2
  4.0 0.7 copy-start.3
  4.6 0.7 copy-start.4

commit v4 on v3

--- a/solution.py
+++ b/solution.py
@@ -7,8 +7,9 @@
 
 HD = 128
 MESH = pl.DeviceIdType.MESH
-PIECES = 8
-LAG = 3
+PIECES = 16
+RELAY_LAG = 3
+LAG = 5
 STACK = 2
 
 
@@ -141,15 +142,14 @@
     own_q.start()
     pl.semaphore_wait(barrier, len(partners))
 
-    def send_weights(k, carry):
+    def send_weights(k):
         w_load(0, k).wait()
         w_load(1, k).wait()
         w_copy(1, k).start()
         w_copy(0, k).start()
-        return carry
-
-    lax.fori_loop(0, PIECES, send_weights, 0)
-
+
+    send_weights(0)
+    send_weights(1)
     index_copy.wait()
     last_copy.wait()
     index_rows = jnp.broadcast_to(index_ref[...], (HD, HD)).T
@@ -160,7 +160,7 @@
             jnp.bfloat16
         )[:, :stop - start]
 
-    def choose(k, carry):
+    def choose(k):
         vision_copy(k).wait()
         picked = jnp.dot(
             onehot[...], vision_buf[lax.rem(k, 2)], preferred_element_type=jnp.float32
@@ -168,14 +168,6 @@
         chosen[k, member] = picked.astype(jnp.bfloat16)
         c_copy(1, k).start()
         c_copy(0, k).start()
-
-        @pl.when(k + 2 < PIECES)
-        def _():
-            vision_copy(k + 2).start()
-
-        return carry
-
-    lax.fori_loop(0, PIECES, choose, 0)
 
     last_all[member] = jnp.broadcast_to(last_ref[...], (8, HD))
     sums[...] = jnp.zeros_like(sums)
@@ -192,15 +184,27 @@
             )
             sums[group] += added.reshape(4, HD, 2 * HD)
 
-    def relay_and_project(k, carry):
+    def relay(k):
+        w_arrival(1, k).wait_recv()
+        w_copy(2, k).start()
+        c_arrival(1, k).wait_recv()
+        c_copy(2, k).start()
+
+    def step_of(k, carry):
         @pl.when(k < PIECES)
         def _():
-            w_arrival(1, k).wait_recv()
-            w_copy(2, k).start()
-            c_arrival(1, k).wait_recv()
-            c_copy(2, k).start()
-
-        @pl.when(k == PIECES - 1)
+            choose(k)
+
+        @pl.when(k + 2 < PIECES)
+        def _():
+            vision_copy(k + 2).start()
+            send_weights(k + 2)
+
+        @pl.when((k >= RELAY_LAG) & (k < PIECES + RELAY_LAG))
+        def _():
+            relay(k - RELAY_LAG)
+
+        @pl.when(k == PIECES + RELAY_LAG - 1)
         def _():
             for t in (1, 2, 3):
                 l_copy(t).start()
@@ -212,7 +216,7 @@
 
         return carry
 
-    lax.fori_loop(0, PIECES + LAG, relay_and_project, 0)
+    lax.fori_loop(0, PIECES + LAG, step_of, 0)
 
     for j in range(4):
         s_copy(j).start()
@@ -368,7 +372,7 @@
             dma((4,)), dma((4,)),
         ],
         compiler_params=pltpu.CompilerParams(
-            collective_id=0, has_side_effects=True, vmem_limit_bytes=46 * 2**20
+            collective_id=0, has_side_effects=True, vmem_limit_bytes=56 * 2**20
         ),
     )(vision, kept_index, w_key.T, w_value.T, queries, last_frame.reshape(1, rows), attn_gate)
 

time: 111 us -> 108 us (0.973)
  local copies, waits for them, and re-layouts: 5.58 us -> 2.29 us
    unnamed x11 -> x1, local copies, waits for them, and re-layouts: 5.58 us -> 2.29 us
where the time goes in v4:
time: 108 us
  Pallas kernels  105 us (97%)
  local copies, waits for them, and re-layouts  2.29 us (2%)
    pallas_call x1, Pallas kernels, fused_local(): pl.pallas_call(fused_kernel, out_shape=jax.ShapeDtypeStruct(queries.shape...  105 us
    unnamed x1, local copies, waits for them, and re-layouts  2.29 us

profile of v4, /device:TPU:0, one launch (start us, length us, event | category | flops | bytes accessed | tf_op | source)
XLA Modules:
  0.0 107.6 jit_solution(12272527990044041140)
XLA Ops:
  0.7 104.6 %shard_map.73 = bf16[128,4096]{1,0:T(8,128)(2,1)} custom-call(bf16[1,1601,4096]{2,1,0:T(8,128)(2,1)} %vision_ref.1, s32[1,128]{1,0:T(1,128)} %index_hbm.1, bf16[64,4096]{1,0:T(8,128)(2,1)} %bitcast.3, bf16[64,4096]{1,0:T(8,128)(2,1)} %bitcast.4, bf16[128,4096]{1,0:T(8,128)(2,1)} %q_ref.1, s32[1,128]{1,0:T(1,128)} %bitcast.5, f32[1]{0:T(128)S(6)} %copy.9.gate_ref), custom_call_target="tpu_custom_call" | custom-call | tf_op jit(solution)/shard_map/pallas_call | solution.py:347
  105.3 2.3 %copy.10 = bf16[128,4096]{1,0:T(8,128)(2,1)} copy(bf16[128,4096]{1,0:T(8,128)(2,1)} %shard_map.73) | data formatting | bytes 2097152

commit v5 on v4

--- a/solution.py
+++ b/solution.py
@@ -10,7 +10,7 @@
 PIECES = 16
 RELAY_LAG = 3
 LAG = 5
-STACK = 2
+STACK = 4
 
 
 def fused_kernel(
@@ -69,11 +69,12 @@
         return send(slot, slot, c_send.at[kind, k], c_recv.at[kind, k], to_y)
 
     def kv_copy(held, send_sem, recv_sem, kind, j):
-        slot = held.at[frame_at(z1 if kind < 2 else 1 - z1, j, x)]
+        slot = held.at[frame_at(z1 if kind < 2 else 1 - z1, j, x), pl.ds(0, HD)]
         return send(slot, slot, send_sem.at[kind, j], recv_sem.at[kind, j], to_z1 if kind == 1 else to_x)
 
     def kv_arrival(held, send_sem, recv_sem, kind, j):
-        slot = held.at[frame_at(z1 if kind == 0 else 1 - z1, j, x if kind == 1 else 1 - x)]
+        frame = frame_at(z1 if kind == 0 else 1 - z1, j, x if kind == 1 else 1 - x)
+        slot = held.at[frame, pl.ds(0, HD)]
         return send(slot, slot, send_sem.at[kind, j], recv_sem.at[kind, j], to_x)
 
     key_part = (keys_all, k_send, k_recv)
@@ -171,6 +172,9 @@
 
     last_all[member] = jnp.broadcast_to(last_ref[...], (8, HD))
     sums[...] = jnp.zeros_like(sums)
+    feature = lax.broadcasted_iota(jnp.int32, (HD, HD), 0)
+    for frame in range(keys_all.shape[0]):
+        keys_all[frame, HD:] = jnp.where(feature == frame, 1.0, 0.0).astype(jnp.bfloat16)
 
     def project(k):
         for kind in (0, 2):
@@ -226,7 +230,7 @@
         key_rows = jnp.concatenate([total[:, :64], total[:, 128:192]], axis=1)
         value_rows = jnp.concatenate([total[:, 64:128], total[:, 192:]], axis=1)
         frame = frame_at(z1, j, x)
-        keys_all[frame] = key_rows.T.astype(jnp.bfloat16)
+        keys_all[frame, 0:HD] = key_rows.T.astype(jnp.bfloat16)
         values_all[frame] = value_rows.astype(jnp.bfloat16)
         kv_copy(*key_part, 1, j).start()
         kv_copy(*key_part, 0, j).start()
@@ -250,7 +254,6 @@
     gate = jnp.tanh(jnp.full((1, HD), gate_ref[0], jnp.float32))
     factor = HD ** (-0.5) * 1.4426950408889634
     steps = width // (STACK * HD)
-    feature = lax.broadcasted_iota(jnp.int32, (HD, HD), 0)
 
     def hidden_of(t):
         last_rows = jnp.broadcast_to(last_all[peer(t), 0:1, :], (HD, HD)).T
@@ -262,13 +265,9 @@
         heads = q_all[peer(t), :, pl.ds(start, STACK * HD)]
         stacked = jnp.concatenate([heads[:, i * HD:(i + 1) * HD] for i in range(STACK)], axis=0)
         key_columns = jnp.concatenate([keys_all[frame] for frame in range(frames)], axis=1)
-        marks = jnp.concatenate(
-            [jnp.where(feature == frame, 1.0, 0.0).astype(jnp.bfloat16) for frame in range(frames)],
-            axis=1,
-        )
         scores = jnp.dot(
             jnp.concatenate([stacked, hidden], axis=1),
-            jnp.concatenate([key_columns, marks], axis=0),
+            key_columns,
             preferred_element_type=jnp.float32,
         )
         row_max = jnp.max(scores, axis=1, keepdims=True)
@@ -358,7 +357,7 @@
             vmem((PIECES, 2, 2, HD, depth), jnp.bfloat16),
             vmem((2, 4, HD, 2 * HD), jnp.float32),
             vmem((4, HD, 2 * HD), jnp.float32),
-            vmem((16, HD, HD), jnp.bfloat16),
+            vmem((16, 2 * HD, HD), jnp.bfloat16),
             vmem((16, HD, HD), jnp.bfloat16),
             vmem((4, rows, width), jnp.bfloat16),
             vmem((4, 8, HD), jnp.int32),

time: 108 us -> 106 us (0.981)
  Pallas kernels: 105 us -> 102 us
    pallas_call x1, Pallas kernels: 105 us -> 102 us  [fused_local(): pl.pallas_call(fused_kernel, out_shape=jax.ShapeDtypeStruct(queries.shape...]
where the time goes in v5:
time: 106 us; the launch traced here: 105 us
  Pallas kernels  102 us (96%)
  local copies, waits for them, and re-layouts  2.29 us (2%)
    pallas_call x1, Pallas kernels, fused_local(): pl.pallas_call(fused_kernel, out_shape=jax.ShapeDtypeStruct(queries.shape...  102 us
    unnamed x1, local copies, waits for them, and re-layouts  2.29 us

profile of v5, /device:TPU:0, one launch (start us, length us, event | category | flops | bytes accessed | tf_op | source)
XLA Modules:
  0.0 105.3 jit_solution(17853343714917827053)
XLA Ops:
  0.7 102.4 %shard_map.73 = bf16[128,4096]{1,0:T(8,128)(2,1)} custom-call(bf16[1,1601,4096]{2,1,0:T(8,128)(2,1)} %vision_ref.1, s32[1,128]{1,0:T(1,128)} %index_hbm.1, bf16[64,4096]{1,0:T(8,128)(2,1)} %bitcast.3, bf16[64,4096]{1,0:T(8,128)(2,1)} %bitcast.4, bf16[128,4096]{1,0:T(8,128)(2,1)} %q_ref.1, s32[1,128]{1,0:T(1,128)} %bitcast.5, f32[1]{0:T(128)S(6)} %copy.9.gate_ref), custom_call_target="tpu_custom_call" | custom-call | tf_op jit(solution)/shard_map/pallas_call | solution.py:346
  103.0 2.3 %copy.10 = bf16[128,4096]{1,0:T(8,128)(2,1)} copy(bf16[128,4096]{1,0:T(8,128)(2,1)} %shard_map.73) | data formatting | bytes 2097152

commit v6 on v5

--- a/solution.py
+++ b/solution.py
@@ -83,7 +83,7 @@
     width = q_all.shape[2]
 
     def peer(t):
-        return lax.rem(member + t, 4)
+        return (1 - z0 if t // 2 else z0) * 2 + (1 - y if t % 2 else y)
 
     def columns_of(m):
         return pl.ds(pl.multiple_of(m * width, width), width)
@@ -93,7 +93,7 @@
         return send(q_ref.at[:, columns_of(peer(t))], q_all.at[member], q_send.at[t], q_recv.at[t], target)
 
     def q_arrival(t):
-        slot = q_all.at[peer(4 - t)]
+        slot = q_all.at[peer(t)]
         return send(slot, slot, q_send.at[t], q_recv.at[t], to_y)
 
     def l_copy(t):
@@ -101,7 +101,7 @@
         return send(last_all.at[member], last_all.at[member], l_send.at[t], l_recv.at[t], target)
 
     def l_arrival(t):
-        slot = last_all.at[peer(4 - t)]
+        slot = last_all.at[peer(t)]
         return send(slot, slot, l_send.at[t], l_recv.at[t], to_y)
 
     def o_copy(t):
@@ -109,7 +109,7 @@
         return send(out_parts.at[t], out_ref.at[:, columns_of(member)], o_send.at[t], o_recv.at[t], target)
 
     def o_arrival(t):
-        slot = out_ref.at[:, columns_of(peer(4 - t))]
+        slot = out_ref.at[:, columns_of(peer(t))]
         return send(slot, slot, o_send.at[t], o_recv.at[t], to_y)
 
     def s_copy(j):
@@ -210,7 +210,7 @@
 
         @pl.when(k == PIECES + RELAY_LAG - 1)
         def _():
-            for t in (1, 2, 3):
+            for t in (3, 2, 1):
                 l_copy(t).start()
                 q_copy(t).start()
 
@@ -296,21 +296,29 @@
 
         lax.fori_loop(0, steps, body, 0)
 
-    own, even, odd = (exps_own, dens_own), (exps_even, dens_even), (exps_odd, dens_odd)
-    run((0, own), None)
-    for t in (1, 2, 3):
+    def queries_here(t):
         l_arrival(t).wait_recv()
         q_arrival(t).wait_recv()
-    run((2, even), None)
+
+    own, even, odd = (exps_own, dens_own), (exps_even, dens_even), (exps_odd, dens_odd)
+    own_hidden = hidden_of(0)
+    for step in range(steps // 2):
+        weigh(0, own_hidden, step, *own)
+    queries_here(3)
+    run((3, even), None)
     for j in range(4):
         kv_arrival(*value_part, 0, j).wait_recv()
         kv_arrival(*value_part, 2, j).wait_recv()
-    run((1, odd), (2, even))
+    queries_here(2)
+    run((2, odd), (3, even))
+    o_copy(3).start()
+    queries_here(1)
+    run((1, even), (2, odd))
     o_copy(2).start()
-    run((3, even), (1, odd))
+    run(None, (1, even))
     o_copy(1).start()
-    run(None, (3, even))
-    o_copy(3).start()
+    for step in range(steps // 2, steps):
+        weigh(0, own_hidden, step, *own)
     run(None, (0, own))
     out_ref[:, columns_of(member)] = out_parts[0]
 

time: 106 us -> 106 us (level)
  no operation moved by 1% of the time
where the time goes in v6:
time: 106 us
  Pallas kernels  103 us (97%)
  local copies, waits for them, and re-layouts  2.29 us (2%)
    pallas_call x1, Pallas kernels, fused_local(): pl.pallas_call(fused_kernel, out_shape=jax.ShapeDtypeStruct(queries.shape...  103 us
    unnamed x1, local copies, waits for them, and re-layouts  2.29 us

profile of v6, /device:TPU:0, one launch (start us, length us, event | category | flops | bytes accessed | tf_op | source)
XLA Modules:
  0.0 105.8 jit_solution(2301781355786931411)
XLA Ops:
  0.7 102.8 %shard_map.73 = bf16[128,4096]{1,0:T(8,128)(2,1)} custom-call(bf16[1,1601,4096]{2,1,0:T(8,128)(2,1)} %vision_ref.1, s32[1,128]{1,0:T(1,128)} %index_hbm.1, bf16[64,4096]{1,0:T(8,128)(2,1)} %bitcast.3, bf16[64,4096]{1,0:T(8,128)(2,1)} %bitcast.4, bf16[128,4096]{1,0:T(8,128)(2,1)} %q_ref.1, s32[1,128]{1,0:T(1,128)} %bitcast.5, f32[1]{0:T(128)S(6)} %copy.9.gate_ref), custom_call_target="tpu_custom_call" | custom-call | tf_op jit(solution)/shard_map/pallas_call | solution.py:354
  103.5 2.3 %copy.10 = bf16[128,4096]{1,0:T(8,128)(2,1)} copy(bf16[128,4096]{1,0:T(8,128)(2,1)} %shard_map.73) | data formatting | bytes 2097152

commit v7 on v6

--- a/solution.py
+++ b/solution.py
@@ -8,8 +8,8 @@
 HD = 128
 MESH = pl.DeviceIdType.MESH
 PIECES = 16
-RELAY_LAG = 3
-LAG = 5
+RELAY_LAG = 2
+LAG = 4
 STACK = 4
 
 

time: 106 us -> 106 us (level)
  no operation moved by 1% of the time
where the time goes in v7:
time: 106 us
  Pallas kernels  103 us (97%)
  local copies, waits for them, and re-layouts  2.29 us (2%)
    pallas_call x1, Pallas kernels, fused_local(): pl.pallas_call(fused_kernel, out_shape=jax.ShapeDtypeStruct(queries.shape...  103 us
    unnamed x1, local copies, waits for them, and re-layouts  2.29 us

profile of v7, /device:TPU:0, one launch (start us, length us, event | category | flops | bytes accessed | tf_op | source)
XLA Modules:
  0.0 105.8 jit_solution(1652903116169283665)
XLA Ops:
  0.7 102.8 %shard_map.73 = bf16[128,4096]{1,0:T(8,128)(2,1)} custom-call(bf16[1,1601,4096]{2,1,0:T(8,128)(2,1)} %vision_ref.1, s32[1,128]{1,0:T(1,128)} %index_hbm.1, bf16[64,4096]{1,0:T(8,128)(2,1)} %bitcast.3, bf16[64,4096]{1,0:T(8,128)(2,1)} %bitcast.4, bf16[128,4096]{1,0:T(8,128)(2,1)} %q_ref.1, s32[1,128]{1,0:T(1,128)} %bitcast.5, f32[1]{0:T(128)S(6)} %copy.9.gate_ref), custom_call_target="tpu_custom_call" | custom-call | tf_op jit(solution)/shard_map/pallas_call | solution.py:354
  103.5 2.3 %copy.10 = bf16[128,4096]{1,0:T(8,128)(2,1)} copy(bf16[128,4096]{1,0:T(8,128)(2,1)} %shard_map.73) | data formatting | bytes 2097152
